TPU v7x, 32 devices: a whole 2x2x4 slice. The times are simulated.
32 devices in a mesh: head: 2 (over x), blk: 16 (over z, y, core).
Axes of the slice: x: 2, y: 2, z: 4, core: 2. Of those that a mesh axis runs over, the one named last changes fastest.
Arguments:
- queries: bfloat16 [2048, 4096], P(('head', 'blk')), may hold values from -6 to 6
- keys: bfloat16 [2048, 1024], P(('head', 'blk')), may hold values from -6 to 6
- values: bfloat16 [2048, 1024], P(('head', 'blk')), may hold values from -6 to 6
- grad_out: bfloat16 [2048, 4096], P(('head', 'blk')), may hold values from -6 to 6
- order: int32 [32], replicated, may hold values from 0 to 31, each once
Outputs:
- grad_queries: bfloat16 [2048, 4096], P(('head', 'blk'))
- grad_keys: bfloat16 [2048, 1024], P(('head', 'blk'))
- grad_values: bfloat16 [2048, 1024], P(('head', 'blk'))
Inputs may be any that keep to these rules, and one draw needn't show every extreme that they name: `order`: each value names one slot's pair of half-blocks, each exactly once.
All inputs are finite; a program needn't handle non-finite values.
Results may differ from a plain program's by a relative error of at most 0.024.
Values may be sent and summed in bfloat16 or wider, within the bound.
A program may use at most 64 MiB of HBM per device.

v0:
```python
import functools
import math

import jax
import jax.numpy as jnp
from jax import lax
from jax.experimental import pallas as pl
from jax.experimental.pallas import tpu as pltpu
from jax.sharding import PartitionSpec as P

MESH = pl.DeviceIdType.MESH
HD = 128
CHUNKS = 4
HIDDEN = -1e30


def rows_dot(left, right):
    return lax.dot_general(
        left, right, (((1,), (1,)), ((), ())), preferred_element_type=jnp.float32
    )


def plain_dot(left, right):
    return jnp.dot(left, right, preferred_element_type=jnp.float32)


def cols_dot(left, right):
    return lax.dot_general(
        left, right, (((0,), (0,)), ((), ())), preferred_element_type=jnp.float32
    )


def kernel(
    n, m, slots, chunks,
    order, q_hbm, k_hbm, v_hbm, g_hbm, dq_hbm, dk_hbm, dv_hbm,
    q, g, dq, kv, part, early, own_grad, prev_out, prev_in, part_out, part_in, result,
    bias_early, bias_other,
    load_sem, part_s, part_r, near_s, near_r, far_s, far_r,
    prev_s, prev_r, late_s, late_r, front_s, front_r, dq_sem, out_sem,
):
    head, blk = lax.axis_index("head"), lax.axis_index("blk")
    rows, key_cols = kv.shape[1], kv.shape[2]
    half = rows // 2
    width = key_cols // chunks
    group = q.shape[1] // key_cols
    lanes = group * half
    heads_in = width // HD
    scale = HD ** -0.5
    ahead = (head, lax.rem(blk + 1, m))
    behind = (head, lax.rem(blk + m - 1, m))
    up = [None] + [(lax.rem(head + d, n), blk) for d in range(1, n)]
    down = [None] + [(lax.rem(head + n - d, n), blk) for d in range(1, n)]

    loads = [
        pltpu.make_async_copy(k_hbm, kv.at[0], load_sem.at[0]),
        pltpu.make_async_copy(v_hbm, kv.at[1], load_sem.at[1]),
        pltpu.make_async_copy(q_hbm, q, load_sem.at[2]),
        pltpu.make_async_copy(g_hbm, g, load_sem.at[3]),
    ]
    for load in loads:
        load.start()

    barrier = pltpu.get_barrier_semaphore()
    for other in up[1:] + [ahead, behind]:
        pl.semaphore_signal(barrier, inc=1, device_id=other, device_id_type=MESH)

    mine = order[head * m + blk]
    row = lax.broadcasted_iota(jnp.int32, (half, lanes), 0)
    col = lax.rem(lax.broadcasted_iota(jnp.int32, (half, lanes), 1), half)
    causal = jnp.where(row <= col, 0.0, HIDDEN)
    blank = jnp.zeros((half, lanes), jnp.float32)
    bias_early[pl.ds(0, half), pl.ds(0, lanes)] = causal
    bias_other[pl.ds(0, half), :] = causal
    for d in range(n):
        bias_early[pl.ds(d * half, half), pl.ds(lanes, lanes)] = blank
        bias_other[pl.ds((n + d) * half, half), :] = blank
        if d > 0:
            theirs = order[lax.rem(head + n - d, n) * m + blk]
            first = jnp.where(theirs < mine, 0.0, HIDDEN)
            bias_early[pl.ds(d * half, half), pl.ds(0, lanes)] = blank + first
            bias_other[pl.ds(d * half, half), :] = blank + (HIDDEN - first)

    def span(c):
        return pl.ds(c * width, width)

    def remote(src, dst, send, recv, where):
        return pltpu.make_async_remote_copy(
            src_ref=src, dst_ref=dst, send_sem=send, recv_sem=recv,
            device_id=where, device_id_type=MESH,
        )

    def to_part(d, c):
        return remote(
            kv.at[:, :, span(c)], part.at[d - 1, :, :, span(c)],
            part_s.at[d - 1, c], part_r.at[d - 1, c], up[d],
        )

    def to_near(c):
        return remote(
            kv.at[:, pl.ds(0, half), span(c)], early.at[0, :, :, span(c)],
            near_s.at[c], near_r.at[c], ahead,
        )

    def to_far(d, c):
        return remote(
            part.at[d - 1, :, pl.ds(0, half), span(c)], early.at[d, :, :, span(c)],
            far_s.at[d - 1, c], far_r.at[d - 1, c], ahead,
        )

    def to_prev(c):
        return remote(
            prev_out.at[:, :, :, span(c)], prev_in.at[:, :, :, span(c)],
            prev_s.at[c], prev_r.at[c], behind,
        )

    def to_late(d, c):
        piece = (d - 1, slice(None), pl.ds(half, half), span(c))
        return remote(
            part_out.at[piece], part_in.at[piece],
            late_s.at[d - 1, c], late_r.at[d - 1, c], down[d],
        )

    def to_front(d, c):
        piece = (d - 1, slice(None), pl.ds(0, half), span(c))
        return remote(
            part_out.at[piece], part_in.at[piece],
            front_s.at[d - 1, c], front_r.at[d - 1, c], down[d],
        )

    def dq_copy(c):
        cols = pl.ds(c * width * group, width * group)
        return pltpu.make_async_copy(dq.at[:, cols], dq_hbm.at[:, cols], dq_sem.at[c])

    def out_copy(i, c):
        target = (dk_hbm, dv_hbm)[i]
        return pltpu.make_async_copy(
            result.at[i, :, span(c)], target.at[:, span(c)], out_sem.at[i, c]
        )

    loads[0].wait()
    loads[1].wait()
    pl.semaphore_wait(barrier, n + 1)
    for c in range(chunks):
        for d in range(1, n):
            to_part(d, c).start()
        to_near(c).start()

    def stacked(array, kv_head):
        cols = [pl.ds((kv_head * group + k) * HD, HD) for k in range(group)]
        return jnp.concatenate(
            [array[pl.ds(0, half), col] for col in cols]
            + [array[pl.ds(half, half), col] for col in cols],
            axis=0,
        )

    def one_head(kv_head):
        cols = pl.ds(kv_head * HD, HD)
        lo, hi = pl.ds(0, half), pl.ds(half, half)

        def sources(i):
            first = [kv[i, lo, cols]] + [part[d - 1, i, lo, cols] for d in range(1, n)]
            rest = [kv[i, hi, cols]] + [part[d - 1, i, hi, cols] for d in range(1, n)]
            rest += [early[d, i, :, cols] for d in range(n)]
            return jnp.concatenate(first, axis=0), jnp.concatenate(rest, axis=0)

        key_first, key_rest = sources(0)
        value_first, value_rest = sources(1)
        queries, grads = stacked(q, kv_head), stacked(g, kv_head)
        late_queries, late_grads = queries[lanes:], grads[lanes:]
        factor = scale * math.log2(math.e)
        logits_first = rows_dot(key_first, queries) * factor + bias_early[...]
        logits_rest = rows_dot(key_rest, late_queries) * factor + bias_other[...]
        spread_first = rows_dot(value_first, grads)
        spread_rest = rows_dot(value_rest, late_grads)

        def both(reduce, combine, first, rest):
            whole = reduce(first, axis=0, keepdims=True)
            tail = combine(whole[:, lanes:], reduce(rest, axis=0, keepdims=True))
            return jnp.concatenate([whole[:, :lanes], tail], axis=1)

        top = both(jnp.max, jnp.maximum, logits_first, logits_rest)
        mass_first = jnp.exp2(logits_first - top)
        mass_rest = jnp.exp2(logits_rest - top[:, lanes:])
        inverse = 1.0 / both(jnp.sum, jnp.add, mass_first, mass_rest)
        weights_first = mass_first * inverse
        weights_rest = mass_rest * inverse[:, lanes:]
        delta = both(
            jnp.sum, jnp.add, weights_first * spread_first, weights_rest * spread_rest
        )
        slopes_first = (weights_first * (spread_first - delta)).astype(jnp.bfloat16)
        slopes_rest = (weights_rest * (spread_rest - delta[:, lanes:])).astype(jnp.bfloat16)
        weights_first = weights_first.astype(jnp.bfloat16)
        weights_rest = weights_rest.astype(jnp.bfloat16)

        query_first = cols_dot(slopes_first, key_first)
        query_rest = cols_dot(slopes_rest, key_rest)
        query_grad = (
            jnp.concatenate([query_first[:lanes], query_first[lanes:] + query_rest], axis=0)
            * scale
        ).astype(jnp.bfloat16)
        for k in range(group):
            out = pl.ds((kv_head * group + k) * HD, HD)
            dq[lo, out] = query_grad[k * half : (k + 1) * half]
            dq[hi, out] = query_grad[lanes + k * half : lanes + (k + 1) * half]
        grads_first = (
            plain_dot(slopes_first, queries) * scale,
            plain_dot(weights_first, grads),
        )
        grads_rest = (
            plain_dot(slopes_rest, late_queries) * scale,
            plain_dot(weights_rest, late_grads),
        )
        for i in range(2):
            own_grad[i, lo, cols] = grads_first[i][:half]
            own_grad[i, hi, cols] = grads_rest[i][:half]
            for d in range(1, n):
                at = d * half
                part_out[d - 1, i, lo, cols] = grads_first[i][at : at + half].astype(jnp.bfloat16)
                part_out[d - 1, i, hi, cols] = grads_rest[i][at : at + half].astype(jnp.bfloat16)
            for d in range(n):
                at = (n + d) * half
                prev_out[d, i, :, cols] = grads_rest[i][at : at + half].astype(jnp.bfloat16)

    def stage_arrive(c):
        for d in range(1, n):
            to_part(d, c).wait_recv()
            to_far(d, c).start()

    def stage_compute(c):
        to_near(c).wait_recv()
        for d in range(1, n):
            to_far(d, c).wait_recv()
        if c == 0:
            loads[2].wait()
            loads[3].wait()
        for index in range(heads_in):
            one_head(c * heads_in + index)
        to_prev(c).start()
        for d in range(1, n):
            to_late(d, c).start()
        dq_copy(c).start()

    def stage_front(c):
        to_prev(c).wait_recv()
        for d in range(1, n):
            for i in range(2):
                spot = (d - 1, i, pl.ds(0, half), span(c))
                total = part_out[spot].astype(jnp.float32)
                total = total + prev_in[d, i, :, span(c)].astype(jnp.float32)
                part_out[spot] = total.astype(jnp.bfloat16)
            to_front(d, c).start()

    def stage_finish(c):
        for d in range(1, n):
            to_late(d, c).wait_recv()
            to_front(d, c).wait_recv()
        for i in range(2):
            total = own_grad[i, :, span(c)]
            for d in range(1, n):
                total = total + part_in[d - 1, i, :, span(c)].astype(jnp.float32)
            front = total[:half] + prev_in[0, i, :, span(c)].astype(jnp.float32)
            result[i, pl.ds(0, half), span(c)] = front.astype(jnp.bfloat16)
            result[i, pl.ds(half, half), span(c)] = total[half:].astype(jnp.bfloat16)
            out_copy(i, c).start()

    for t in range(chunks + 2):
        if t < chunks:
            stage_arrive(t)
        if 0 <= t - 1 < chunks:
            stage_compute(t - 1)
        if 0 <= t - 2 < chunks:
            stage_front(t - 2)
    for c in range(chunks):
        stage_finish(c)
    for c in range(chunks):
        to_near(c).wait_send()
        to_prev(c).wait_send()
        for d in range(1, n):
            to_part(d, c).wait_send()
            to_far(d, c).wait_send()
            to_late(d, c).wait_send()
            to_front(d, c).wait_send()
        dq_copy(c).wait()
        out_copy(0, c).wait()
        out_copy(1, c).wait()


def solution(mesh):
    n, m = mesh.shape["head"], mesh.shape["blk"]

    def body(queries, keys, values, grad_out, order):
        rows, query_cols = queries.shape
        key_cols = keys.shape[1]
        half = rows // 2
        chunks = min(CHUNKS, key_cols // HD)
        lanes = half * (query_cols // key_cols)
        low, wide = jnp.bfloat16, jnp.float32
        dma = pltpu.SemaphoreType.DMA
        anywhere = pl.BlockSpec(memory_space=pl.ANY)
        return pl.pallas_call(
            functools.partial(kernel, n, m, order.shape[0], chunks),
            out_shape=(
                jax.ShapeDtypeStruct(queries.shape, low),
                jax.ShapeDtypeStruct(keys.shape, low),
                jax.ShapeDtypeStruct(values.shape, low),
            ),
            in_specs=[pl.BlockSpec(memory_space=pltpu.SMEM)] + [anywhere] * 4,
            out_specs=[anywhere] * 3,
            scratch_shapes=[
                pltpu.VMEM((rows, query_cols), low),
                pltpu.VMEM((rows, query_cols), low),
                pltpu.VMEM((rows, query_cols), low),
                pltpu.VMEM((2, rows, key_cols), low),
                pltpu.VMEM((n - 1, 2, rows, key_cols), low),
                pltpu.VMEM((n, 2, half, key_cols), low),
                pltpu.VMEM((2, rows, key_cols), wide),
                pltpu.VMEM((n, 2, half, key_cols), low),
                pltpu.VMEM((n, 2, half, key_cols), low),
                pltpu.VMEM((n - 1, 2, rows, key_cols), low),
                pltpu.VMEM((n - 1, 2, rows, key_cols), low),
                pltpu.VMEM((2, rows, key_cols), low),
                pltpu.VMEM((n * half, 2 * lanes), wide),
                pltpu.VMEM((2 * n * half, lanes), wide),
                dma((4,)),
                dma((n - 1, chunks)), dma((n - 1, chunks)),
                dma((chunks,)), dma((chunks,)),
                dma((n - 1, chunks)), dma((n - 1, chunks)),
                dma((chunks,)), dma((chunks,)),
                dma((n - 1, chunks)), dma((n - 1, chunks)),
                dma((n - 1, chunks)), dma((n - 1, chunks)),
                dma((chunks,)), dma((2, chunks)),
            ],
            compiler_params=pltpu.CompilerParams(
                collective_id=0, has_side_effects=True, vmem_limit_bytes=40 * 2**20
            ),
        )(order, queries, keys, values, grad_out)

    shard = P(("head", "blk"), None)
    return jax.shard_map(
        body,
        mesh=mesh,
        in_specs=(shard, shard, shard, shard, P()),
        out_specs=(shard, shard, shard),
        check_vma=False,
    )
```

profile of v0, /device:TPU:0, one launch (start us, length us, event | category | flops | bytes accessed | tf_op | source)
XLA Modules:
  0.0 33.2 jit_solution(7610539650122694440)
XLA Ops:
  0.6 0.0 copy-start
  0.6 1.0 %copy-done = bf16[64,4096]{1,0:T(8,128)(2,1)S(1)} copy-done((bf16[64,4096]{1,0:T(8,128)(2,1)S(1)}, bf16[64,4096]{1,0:T(8,128)(2,1)}, u32[]{:S(2)}) %copy-start) | copy-done | bytes 524312
  1.7 0.0 copy-start.1
  1.7 1.0 %copy-done.1 = bf16[64,4096]{1,0:T(8,128)(2,1)S(1)} copy-done((bf16[64,4096]{1,0:T(8,128)(2,1)S(1)}, bf16[64,4096]{1,0:T(8,128)(2,1)}, u32[]{:S(2)}) %copy-start.1) | copy-done | bytes 524312
  2.7 0.0 copy-start.2
  2.7 0.9 %copy-done.2 = bf16[64,1024]{1,0:T(8,128)(2,1)S(1)} copy-done((bf16[64,1024]{1,0:T(8,128)(2,1)S(1)}, bf16[64,1024]{1,0:T(8,128)(2,1)}, u32[]{:S(2)}) %copy-start.2) | copy-done | bytes 131096
  3.6 0.0 copy-start.3
  3.6 0.9 %copy-done.3 = bf16[64,1024]{1,0:T(8,128)(2,1)S(1)} copy-done((bf16[64,1024]{1,0:T(8,128)(2,1)S(1)}, bf16[64,1024]{1,0:T(8,128)(2,1)}, u32[]{:S(2)}) %copy-start.3) | copy-done | bytes 131096
  4.5 0.0 copy-start.4
  4.5 0.7 %copy-done.4 = s32[32]{0:T(128)S(1)} copy-done((s32[32]{0:T(128)S(1)}, s32[32]{0:T(128)}, u32[]{:S(2)}) %copy-start.4) | copy-done | bytes 152
  5.2 25.9 %shard_map.76 = (bf16[64,4096]{1,0:T(8,128)(2,1)S(1)}, bf16[64,1024]{1,0:T(8,128)(2,1)S(1)}, bf16[64,1024]{1,0:T(8,128)(2,1)S(1)}) custom-call(s32[32]{0:T(128)S(1)} %copy-done.4, bf16[64,4096]{1,0:T(8,128)(2,1)S(1)} %copy-done, bf16[64,1024]{1,0:T(8,128)(2,1)S(1)} %copy-done.2, bf16[64,1024]{1,0:T(8,128)(2,1)S(1)} %copy-done.3, bf16[64,4096]{1,0:T(8,128)(2,1)S(1)} %copy-done.1), custom_call_target="tpu_custom_call" | custom-call | tf_op jit(solution)/shard_map/pallas_call | solution.py:300
  31.1 0.8 %copy.11 = bf16[64,4096]{1,0:T(8,128)(2,1)} copy(bf16[64,4096]{1,0:T(8,128)(2,1)S(1)} %get-tuple-element.6) | data formatting | bytes 1048576
  31.9 0.7 %copy.12 = bf16[64,1024]{1,0:T(8,128)(2,1)} copy(bf16[64,1024]{1,0:T(8,128)(2,1)S(1)} %get-tuple-element.7) | data formatting | bytes 262144
  32.6 0.7 %copy.13 = bf16[64,1024]{1,0:T(8,128)(2,1)} copy(bf16[64,1024]{1,0:T(8,128)(2,1)S(1)} %get-tuple-element.8) | data formatting | bytes 262144
Async XLA Ops:
  0.6 1.0 %copy-start = (bf16[64,4096]{1,0:T(8,128)(2,1)S(1)}, bf16[64,4096]{1,0:T(8,128)(2,1)}, u32[]{:S(2)}) copy-start(bf16[64,4096]{1,0:T(8,128)(2,1)} %q_hbm.1) | copy-start | bytes 1572868
  1.7 1.0 %copy-start.1 = (bf16[64,4096]{1,0:T(8,128)(2,1)S(1)}, bf16[64,4096]{1,0:T(8,128)(2,1)}, u32[]{:S(2)}) copy-start(bf16[64,4096]{1,0:T(8,128)(2,1)} %g_hbm.1) | copy-start | bytes 1572868
  2.7 0.9 %copy-start.2 = (bf16[64,1024]{1,0:T(8,128)(2,1)S(1)}, bf16[64,1024]{1,0:T(8,128)(2,1)}, u32[]{:S(2)}) copy-start(bf16[64,1024]{1,0:T(8,128)(2,1)} %k_hbm.1) | copy-start | bytes 393220
  3.6 0.9 %copy-start.3 = (bf16[64,1024]{1,0:T(8,128)(2,1)S(1)}, bf16[64,1024]{1,0:T(8,128)(2,1)}, u32[]{:S(2)}) copy-start(bf16[64,1024]{1,0:T(8,128)(2,1)} %v_hbm.1) | copy-start | bytes 393220
  4.5 0.7 %copy-start.4 = (s32[32]{0:T(128)S(1)}, s32[32]{0:T(128)}, u32[]{:S(2)}) copy-start(s32[32]{0:T(128)} %order.1) | copy-start | bytes 388
where the time goes:
time: 33.5 us; the launch traced here: 33.2 us
  Pallas kernels  25.9 us (77%)
  local copies, waits for them, and re-layouts  6.64 us (20%)
  between operations  0.65 us (2%)
    pallas_call x1, Pallas kernels, body(): pl.pallas_call(functools.partial(kernel, n, m, order.shape[0], chunks), o...  25.9 us
    unnamed x13, local copies, waits for them, and re-layouts  6.64 us

commit v1 on v0

--- a/solution.py
+++ b/solution.py
@@ -32,10 +32,10 @@
 
 def kernel(
     n, m, slots, chunks,
-    order, q_hbm, k_hbm, v_hbm, g_hbm, dq_hbm, dk_hbm, dv_hbm,
+    order_hbm, q_hbm, k_hbm, v_hbm, g_hbm, dq_hbm, dk_hbm, dv_hbm,
     q, g, dq, kv, part, early, own_grad, prev_out, prev_in, part_out, part_in, result,
-    bias_early, bias_other,
-    load_sem, part_s, part_r, near_s, near_r, far_s, far_r,
+    bias_early, bias_other, order,
+    load_sem, head_s, head_r, tail_s, tail_r, near_s, near_r, far_s, far_r,
     prev_s, prev_r, late_s, late_r, front_s, front_r, dq_sem, out_sem,
 ):
     head, blk = lax.axis_index("head"), lax.axis_index("blk")
@@ -56,6 +56,7 @@
         pltpu.make_async_copy(v_hbm, kv.at[1], load_sem.at[1]),
         pltpu.make_async_copy(q_hbm, q, load_sem.at[2]),
         pltpu.make_async_copy(g_hbm, g, load_sem.at[3]),
+        pltpu.make_async_copy(order_hbm, order, load_sem.at[4]),
     ]
     for load in loads:
         load.start()
@@ -64,6 +65,74 @@
     for other in up[1:] + [ahead, behind]:
         pl.semaphore_signal(barrier, inc=1, device_id=other, device_id_type=MESH)
 
+    def span(c):
+        return pl.ds(c * width, width)
+
+    def remote(src, dst, send, recv, where):
+        return pltpu.make_async_remote_copy(
+            src_ref=src, dst_ref=dst, send_sem=send, recv_sem=recv,
+            device_id=where, device_id_type=MESH,
+        )
+
+    def to_part(d, c, late):
+        piece = (slice(None), pl.ds(half if late else 0, half), span(c))
+        sends, recvs = (tail_s, tail_r) if late else (head_s, head_r)
+        return remote(
+            kv.at[piece], part.at[(d - 1,) + piece],
+            sends.at[d - 1, c], recvs.at[d - 1, c], up[d],
+        )
+
+    def to_near(c):
+        return remote(
+            kv.at[:, pl.ds(0, half), span(c)], early.at[0, :, :, span(c)],
+            near_s.at[c], near_r.at[c], ahead,
+        )
+
+    def to_far(d, c):
+        return remote(
+            part.at[d - 1, :, pl.ds(0, half), span(c)], early.at[d, :, :, span(c)],
+            far_s.at[d - 1, c], far_r.at[d - 1, c], ahead,
+        )
+
+    def to_prev(c):
+        return remote(
+            prev_out.at[:, :, :, span(c)], prev_in.at[:, :, :, span(c)],
+            prev_s.at[c], prev_r.at[c], behind,
+        )
+
+    def to_late(d, c):
+        piece = (d - 1, slice(None), pl.ds(half, half), span(c))
+        return remote(
+            part_out.at[piece], part_in.at[piece],
+            late_s.at[d - 1, c], late_r.at[d - 1, c], down[d],
+        )
+
+    def to_front(d, c):
+        piece = (d - 1, slice(None), pl.ds(0, half), span(c))
+        return remote(
+            part_out.at[piece], part_in.at[piece],
+            front_s.at[d - 1, c], front_r.at[d - 1, c], down[d],
+        )
+
+    def dq_copy(c):
+        cols = pl.ds(c * width * group, width * group)
+        return pltpu.make_async_copy(dq.at[:, cols], dq_hbm.at[:, cols], dq_sem.at[c])
+
+    def out_copy(i, c):
+        target = (dk_hbm, dv_hbm)[i]
+        return pltpu.make_async_copy(
+            result.at[i, :, span(c)], target.at[:, span(c)], out_sem.at[i, c]
+        )
+
+    loads[0].wait()
+    loads[1].wait()
+    pl.semaphore_wait(barrier, n + 1)
+    for c in range(chunks):
+        for d in range(1, n):
+            to_part(d, c, False).start()
+        to_near(c).start()
+
+    loads[4].wait()
     mine = order[head * m + blk]
     row = lax.broadcasted_iota(jnp.int32, (half, lanes), 0)
     col = lax.rem(lax.broadcasted_iota(jnp.int32, (half, lanes), 1), half)
@@ -80,71 +149,6 @@
             bias_early[pl.ds(d * half, half), pl.ds(0, lanes)] = blank + first
             bias_other[pl.ds(d * half, half), :] = blank + (HIDDEN - first)
 
-    def span(c):
-        return pl.ds(c * width, width)
-
-    def remote(src, dst, send, recv, where):
-        return pltpu.make_async_remote_copy(
-            src_ref=src, dst_ref=dst, send_sem=send, recv_sem=recv,
-            device_id=where, device_id_type=MESH,
-        )
-
-    def to_part(d, c):
-        return remote(
-            kv.at[:, :, span(c)], part.at[d - 1, :, :, span(c)],
-            part_s.at[d - 1, c], part_r.at[d - 1, c], up[d],
-        )
-
-    def to_near(c):
-        return remote(
-            kv.at[:, pl.ds(0, half), span(c)], early.at[0, :, :, span(c)],
-            near_s.at[c], near_r.at[c], ahead,
-        )
-
-    def to_far(d, c):
-        return remote(
-            part.at[d - 1, :, pl.ds(0, half), span(c)], early.at[d, :, :, span(c)],
-            far_s.at[d - 1, c], far_r.at[d - 1, c], ahead,
-        )
-
-    def to_prev(c):
-        return remote(
-            prev_out.at[:, :, :, span(c)], prev_in.at[:, :, :, span(c)],
-            prev_s.at[c], prev_r.at[c], behind,
-        )
-
-    def to_late(d, c):
-        piece = (d - 1, slice(None), pl.ds(half, half), span(c))
-        return remote(
-            part_out.at[piece], part_in.at[piece],
-            late_s.at[d - 1, c], late_r.at[d - 1, c], down[d],
-        )
-
-    def to_front(d, c):
-        piece = (d - 1, slice(None), pl.ds(0, half), span(c))
-        return remote(
-            part_out.at[piece], part_in.at[piece],
-            front_s.at[d - 1, c], front_r.at[d - 1, c], down[d],
-        )
-
-    def dq_copy(c):
-        cols = pl.ds(c * width * group, width * group)
-        return pltpu.make_async_copy(dq.at[:, cols], dq_hbm.at[:, cols], dq_sem.at[c])
-
-    def out_copy(i, c):
-        target = (dk_hbm, dv_hbm)[i]
-        return pltpu.make_async_copy(
-            result.at[i, :, span(c)], target.at[:, span(c)], out_sem.at[i, c]
-        )
-
-    loads[0].wait()
-    loads[1].wait()
-    pl.semaphore_wait(barrier, n + 1)
-    for c in range(chunks):
-        for d in range(1, n):
-            to_part(d, c).start()
-        to_near(c).start()
-
     def stacked(array, kv_head):
         cols = [pl.ds((kv_head * group + k) * HD, HD) for k in range(group)]
         return jnp.concatenate(
@@ -223,13 +227,15 @@
 
     def stage_arrive(c):
         for d in range(1, n):
-            to_part(d, c).wait_recv()
+            to_part(d, c, False).wait_recv()
             to_far(d, c).start()
+            to_part(d, c, True).start()
 
     def stage_compute(c):
         to_near(c).wait_recv()
         for d in range(1, n):
             to_far(d, c).wait_recv()
+            to_part(d, c, True).wait_recv()
         if c == 0:
             loads[2].wait()
             loads[3].wait()
@@ -263,26 +269,37 @@
             result[i, pl.ds(half, half), span(c)] = total[half:].astype(jnp.bfloat16)
             out_copy(i, c).start()
 
-    for t in range(chunks + 2):
-        if t < chunks:
-            stage_arrive(t)
-        if 0 <= t - 1 < chunks:
-            stage_compute(t - 1)
-        if 0 <= t - 2 < chunks:
-            stage_front(t - 2)
+    for stage in (stage_arrive, stage_compute, stage_front):
+        for c in range(chunks):
+            stage(c)
     for c in range(chunks):
         stage_finish(c)
     for c in range(chunks):
         to_near(c).wait_send()
         to_prev(c).wait_send()
         for d in range(1, n):
-            to_part(d, c).wait_send()
+            to_part(d, c, False).wait_send()
+            to_part(d, c, True).wait_send()
             to_far(d, c).wait_send()
             to_late(d, c).wait_send()
             to_front(d, c).wait_send()
         dq_copy(c).wait()
         out_copy(0, c).wait()
         out_copy(1, c).wait()
+
+
+def hand_over(a, b, c, a_out, b_out, c_out, sem):
+    rows = a.shape[0] // 4
+    pairs = [(b, b_out), (c, c_out)]
+    for i in range(4):
+        pairs.append((a.at[pl.ds(i * rows, rows)], a_out.at[pl.ds(i * rows, rows)]))
+    copies = [
+        pltpu.make_async_copy(src, dst, sem.at[i]) for i, (src, dst) in enumerate(pairs)
+    ]
+    for copy in copies:
+        copy.start()
+    for copy in copies:
+        copy.wait()
 
 
 def solution(mesh):
@@ -297,14 +314,14 @@
         low, wide = jnp.bfloat16, jnp.float32
         dma = pltpu.SemaphoreType.DMA
         anywhere = pl.BlockSpec(memory_space=pl.ANY)
-        return pl.pallas_call(
+        grads = pl.pallas_call(
             functools.partial(kernel, n, m, order.shape[0], chunks),
             out_shape=(
                 jax.ShapeDtypeStruct(queries.shape, low),
                 jax.ShapeDtypeStruct(keys.shape, low),
                 jax.ShapeDtypeStruct(values.shape, low),
             ),
-            in_specs=[pl.BlockSpec(memory_space=pltpu.SMEM)] + [anywhere] * 4,
+            in_specs=[anywhere] * 5,
             out_specs=[anywhere] * 3,
             scratch_shapes=[
                 pltpu.VMEM((rows, query_cols), low),
@@ -321,7 +338,9 @@
                 pltpu.VMEM((2, rows, key_cols), low),
                 pltpu.VMEM((n * half, 2 * lanes), wide),
                 pltpu.VMEM((2 * n * half, lanes), wide),
-                dma((4,)),
+                pltpu.SMEM(order.shape, order.dtype),
+                dma((5,)),
+                dma((n - 1, chunks)), dma((n - 1, chunks)),
                 dma((n - 1, chunks)), dma((n - 1, chunks)),
                 dma((chunks,)), dma((chunks,)),
                 dma((n - 1, chunks)), dma((n - 1, chunks)),
@@ -331,9 +350,17 @@
                 dma((chunks,)), dma((2, chunks)),
             ],
             compiler_params=pltpu.CompilerParams(
-                collective_id=0, has_side_effects=True, vmem_limit_bytes=40 * 2**20
+                collective_id=0, has_side_effects=True, vmem_limit_bytes=64 * 2**20 - 2**16
             ),
         )(order, queries, keys, values, grad_out)
+        return pl.pallas_call(
+            hand_over,
+            out_shape=tuple(jax.ShapeDtypeStruct(x.shape, x.dtype) for x in grads),
+            in_specs=[anywhere] * 3,
+            out_specs=[anywhere] * 3,
+            scratch_shapes=[dma((6,))],
+            compiler_params=pltpu.CompilerParams(vmem_limit_bytes=64 * 2**20 - 2**16),
+        )(*grads)
 
     shard = P(("head", "blk"), None)
     return jax.shard_map(

time: 33.5 us -> 46.8 us (1.40)
  Pallas kernels: 25.9 us -> 46.1 us
  local copies, waits for them, and re-layouts: 6.64 us -> 0 us
    pallas_call x0 -> x1, Pallas kernels: none -> 25 us  [body(): pl.pallas_call(hand_over, out_shape=tuple((jax.ShapeDtypeStruct(x.shape,...]
    unnamed x13 -> x0, local copies, waits for them, and re-layouts: 6.64 us -> none
    pallas_call x1, Pallas kernels: 25.9 us -> 21.1 us  [body(): pl.pallas_call(functools.partial(kernel, n, m, order.shape[0], chunks), o...]
where the time goes in v1:
time: 46.8 us; the launch traced here: 46.7 us
  Pallas kernels  46.1 us (99%)
  between operations  0.64 us (1%)
    pallas_call x1, Pallas kernels, body(): pl.pallas_call(hand_over, out_shape=tuple((jax.ShapeDtypeStruct(x.shape,...  25 us
    pallas_call x1, Pallas kernels, body(): pl.pallas_call(functools.partial(kernel, n, m, order.shape[0], chunks), o...  21.1 us

profile of v1, /device:TPU:0, one launch (start us, length us, event | category | flops | bytes accessed | tf_op | source)
XLA Modules:
  0.0 46.7 jit_solution(12799928590937208871)
XLA Ops:
  0.6 21.1 %shard_map.76 = (bf16[64,4096]{1,0:T(8,128)(2,1)}, bf16[64,1024]{1,0:T(8,128)(2,1)}, bf16[64,1024]{1,0:T(8,128)(2,1)}) custom-call(s32[32]{0:T(128)} %order_hbm.1, bf16[64,4096]{1,0:T(8,128)(2,1)} %q_hbm.1, bf16[64,1024]{1,0:T(8,128)(2,1)} %k_hbm.1, bf16[64,1024]{1,0:T(8,128)(2,1)} %v_hbm.1, bf16[64,4096]{1,0:T(8,128)(2,1)} %g_hbm.1), custom_call_target="tpu_custom_call" | custom-call | tf_op jit(solution)/shard_map/pallas_call | solution.py:317
  21.7 25.0 %shard_map.77 = (bf16[64,4096]{1,0:T(8,128)(2,1)}, bf16[64,1024]{1,0:T(8,128)(2,1)}, bf16[64,1024]{1,0:T(8,128)(2,1)}) custom-call(bf16[64,4096]{1,0:T(8,128)(2,1)} %get-tuple-element.6.a, bf16[64,1024]{1,0:T(8,128)(2,1)} %get-tuple-element.7.b, bf16[64,1024]{1,0:T(8,128)(2,1)} %get-tuple-element.8.c), custom_call_target="tpu_custom_call" | custom-call | tf_op jit(solution)/shard_map/pallas_call | solution.py:356

commit v2 on v1

--- a/solution.py
+++ b/solution.py
@@ -350,16 +350,19 @@
                 dma((chunks,)), dma((2, chunks)),
             ],
             compiler_params=pltpu.CompilerParams(
-                collective_id=0, has_side_effects=True, vmem_limit_bytes=64 * 2**20 - 2**16
+                collective_id=0, has_side_effects=True, vmem_limit_bytes=40 * 2**20
             ),
-        )(order, queries, keys, values, grad_out)
+        )(*(
+            pltpu.with_memory_space_constraint(x, pltpu.HBM)
+            for x in (order, queries, keys, values, grad_out)
+        ))
         return pl.pallas_call(
             hand_over,
             out_shape=tuple(jax.ShapeDtypeStruct(x.shape, x.dtype) for x in grads),
             in_specs=[anywhere] * 3,
             out_specs=[anywhere] * 3,
             scratch_shapes=[dma((6,))],
-            compiler_params=pltpu.CompilerParams(vmem_limit_bytes=64 * 2**20 - 2**16),
+            compiler_params=pltpu.CompilerParams(vmem_limit_bytes=2**20),
         )(*grads)
 
     shard = P(("head", "blk"), None)

time: 46.8 us -> 22.3 us (0.48)
  Pallas kernels: 46.1 us -> 21.5 us
    pallas_call x1, Pallas kernels: 25 us -> 0.92 us  [body(): pl.pallas_call(hand_over, out_shape=tuple((jax.ShapeDtypeStruct(x.shape,...]
where the time goes in v2:
time: 22.3 us; the launch traced here: 22.2 us
  Pallas kernels  21.5 us (96%)
  between operations  0.64 us (3%)
    pallas_call x1, Pallas kernels, body(): pl.pallas_call(functools.partial(kernel, n, m, order.shape[0], chunks), o...  20.6 us
    pallas_call x1, Pallas kernels, body(): pl.pallas_call(hand_over, out_shape=tuple((jax.ShapeDtypeStruct(x.shape,...  0.92 us

profile of v2, /device:TPU:0, one launch (start us, length us, event | category | flops | bytes accessed | tf_op | source)
XLA Modules:
  0.0 22.2 jit_solution(15883975836996253399)
XLA Ops:
  0.6 20.6 %shard_map.76 = (bf16[64,4096]{1,0:T(8,128)(2,1)S(1)}, bf16[64,1024]{1,0:T(8,128)(2,1)S(1)}, bf16[64,1024]{1,0:T(8,128)(2,1)S(1)}) custom-call(s32[32]{0:T(128)} %order_hbm.1, bf16[64,4096]{1,0:T(8,128)(2,1)} %q_hbm.1, bf16[64,1024]{1,0:T(8,128)(2,1)} %k_hbm.1, bf16[64,1024]{1,0:T(8,128)(2,1)} %v_hbm.1, bf16[64,4096]{1,0:T(8,128)(2,1)} %g_hbm.1), custom_call_target="tpu_custom_call" | custom-call | tf_op jit(solution)/shard_map/pallas_call | solution.py:317
  21.3 0.9 %shard_map.77 = (bf16[64,4096]{1,0:T(8,128)(2,1)}, bf16[64,1024]{1,0:T(8,128)(2,1)}, bf16[64,1024]{1,0:T(8,128)(2,1)}) custom-call(bf16[64,4096]{1,0:T(8,128)(2,1)S(1)} %get-tuple-element.6.a, bf16[64,1024]{1,0:T(8,128)(2,1)S(1)} %get-tuple-element.7.b, bf16[64,1024]{1,0:T(8,128)(2,1)S(1)} %get-tuple-element.8.c), custom_call_target="tpu_custom_call" | custom-call | tf_op jit(solution)/shard_map/pallas_call | solution.py:359

commit v3 on v2

--- a/solution.py
+++ b/solution.py
@@ -34,7 +34,7 @@
     n, m, slots, chunks,
     order_hbm, q_hbm, k_hbm, v_hbm, g_hbm, dq_hbm, dk_hbm, dv_hbm,
     q, g, dq, kv, part, early, own_grad, prev_out, prev_in, part_out, part_in, result,
-    bias_early, bias_other, order,
+    bias_early, bias_other, order, ready,
     load_sem, head_s, head_r, tail_s, tail_r, near_s, near_r, far_s, far_r,
     prev_s, prev_r, late_s, late_r, front_s, front_r, dq_sem, out_sem,
 ):
@@ -157,24 +157,32 @@
             axis=0,
         )
 
+    lo, hi = pl.ds(0, half), pl.ds(half, half)
+    factor = scale * math.log2(math.e)
+
+    def early_keys(i, cols):
+        first = [kv[i, lo, cols]] + [part[d - 1, i, lo, cols] for d in range(1, n)]
+        return jnp.concatenate(first, axis=0)
+
+    def other_keys(i, cols):
+        rest = [kv[i, hi, cols]] + [part[d - 1, i, hi, cols] for d in range(1, n)]
+        rest += [early[d, i, :, cols] for d in range(n)]
+        return jnp.concatenate(rest, axis=0)
+
+    def first_logits(kv_head):
+        cols = pl.ds(kv_head * HD, HD)
+        logits = rows_dot(early_keys(0, cols), stacked(q, kv_head))
+        ready[kv_head, 0] = logits * factor + bias_early[...]
+        ready[kv_head, 1] = rows_dot(early_keys(1, cols), stacked(g, kv_head))
+
     def one_head(kv_head):
         cols = pl.ds(kv_head * HD, HD)
-        lo, hi = pl.ds(0, half), pl.ds(half, half)
-
-        def sources(i):
-            first = [kv[i, lo, cols]] + [part[d - 1, i, lo, cols] for d in range(1, n)]
-            rest = [kv[i, hi, cols]] + [part[d - 1, i, hi, cols] for d in range(1, n)]
-            rest += [early[d, i, :, cols] for d in range(n)]
-            return jnp.concatenate(first, axis=0), jnp.concatenate(rest, axis=0)
-
-        key_first, key_rest = sources(0)
-        value_first, value_rest = sources(1)
+        key_first, key_rest = early_keys(0, cols), other_keys(0, cols)
+        value_rest = other_keys(1, cols)
         queries, grads = stacked(q, kv_head), stacked(g, kv_head)
         late_queries, late_grads = queries[lanes:], grads[lanes:]
-        factor = scale * math.log2(math.e)
-        logits_first = rows_dot(key_first, queries) * factor + bias_early[...]
+        logits_first, spread_first = ready[kv_head, 0], ready[kv_head, 1]
         logits_rest = rows_dot(key_rest, late_queries) * factor + bias_other[...]
-        spread_first = rows_dot(value_first, grads)
         spread_rest = rows_dot(value_rest, late_grads)
 
         def both(reduce, combine, first, rest):
@@ -230,15 +238,17 @@
             to_part(d, c, False).wait_recv()
             to_far(d, c).start()
             to_part(d, c, True).start()
-
-    def stage_compute(c):
-        to_near(c).wait_recv()
-        for d in range(1, n):
-            to_far(d, c).wait_recv()
-            to_part(d, c, True).wait_recv()
         if c == 0:
             loads[2].wait()
             loads[3].wait()
+        for index in range(heads_in):
+            first_logits(c * heads_in + index)
+
+    def stage_compute(c):
+        to_near(c).wait_recv()
+        for d in range(1, n):
+            to_far(d, c).wait_recv()
+            to_part(d, c, True).wait_recv()
         for index in range(heads_in):
             one_head(c * heads_in + index)
         to_prev(c).start()
@@ -269,9 +279,13 @@
             result[i, pl.ds(half, half), span(c)] = total[half:].astype(jnp.bfloat16)
             out_copy(i, c).start()
 
-    for stage in (stage_arrive, stage_compute, stage_front):
-        for c in range(chunks):
-            stage(c)
+    for c in range(chunks):
+        stage_arrive(c)
+    for t in range(chunks + 2):
+        if t < chunks:
+            stage_compute(t)
+        if t >= 2:
+            stage_front(t - 2)
     for c in range(chunks):
         stage_finish(c)
     for c in range(chunks):
@@ -339,6 +353,7 @@
                 pltpu.VMEM((n * half, 2 * lanes), wide),
                 pltpu.VMEM((2 * n * half, lanes), wide),
                 pltpu.SMEM(order.shape, order.dtype),
+                pltpu.VMEM((key_cols // HD, 2, n * half, 2 * lanes), wide),
                 dma((5,)),
                 dma((n - 1, chunks)), dma((n - 1, chunks)),
                 dma((n - 1, chunks)), dma((n - 1, chunks)),

time: 22.3 us -> 22.2 us (level)
  no operation moved by 1% of the time
where the time goes in v3:
time: 22.2 us; the launch traced here: 22.1 us
  Pallas kernels  21.4 us (96%)
  between operations  0.64 us (3%)
    pallas_call x1, Pallas kernels, body(): pl.pallas_call(functools.partial(kernel, n, m, order.shape[0], chunks), o...  20.5 us
    pallas_call x1, Pallas kernels, body(): pl.pallas_call(hand_over, out_shape=tuple((jax.ShapeDtypeStruct(x.shape,...  0.92 us

profile of v3, /device:TPU:0, one launch (start us, length us, event | category | flops | bytes accessed | tf_op | source)
XLA Modules:
  0.0 22.1 jit_solution(8532229272913157857)
XLA Ops:
  0.6 20.5 %shard_map.76 = (bf16[64,4096]{1,0:T(8,128)(2,1)S(1)}, bf16[64,1024]{1,0:T(8,128)(2,1)S(1)}, bf16[64,1024]{1,0:T(8,128)(2,1)S(1)}) custom-call(s32[32]{0:T(128)} %order_hbm.1, bf16[64,4096]{1,0:T(8,128)(2,1)} %q_hbm.1, bf16[64,1024]{1,0:T(8,128)(2,1)} %k_hbm.1, bf16[64,1024]{1,0:T(8,128)(2,1)} %v_hbm.1, bf16[64,4096]{1,0:T(8,128)(2,1)} %g_hbm.1), custom_call_target="tpu_custom_call" | custom-call | tf_op jit(solution)/shard_map/pallas_call | solution.py:331
  21.1 0.9 %shard_map.77 = (bf16[64,4096]{1,0:T(8,128)(2,1)}, bf16[64,1024]{1,0:T(8,128)(2,1)}, bf16[64,1024]{1,0:T(8,128)(2,1)}) custom-call(bf16[64,4096]{1,0:T(8,128)(2,1)S(1)} %get-tuple-element.6.a, bf16[64,1024]{1,0:T(8,128)(2,1)S(1)} %get-tuple-element.7.b, bf16[64,1024]{1,0:T(8,128)(2,1)S(1)} %get-tuple-element.8.c), custom_call_target="tpu_custom_call" | custom-call | tf_op jit(solution)/shard_map/pallas_call | solution.py:374

commit v4 on v3

--- a/solution.py
+++ b/solution.py
@@ -10,7 +10,7 @@
 
 MESH = pl.DeviceIdType.MESH
 HD = 128
-CHUNKS = 4
+CHUNKS = 8
 HIDDEN = -1e30
 
 

time: 22.2 us -> 22.9 us (1.032)
  the two profiles are of different devices: /device:TPU:0 before, /device:TPU:25 now
where the time goes in v4:
time: 22.9 us; the launch traced here: 22.8 us
  Pallas kernels  22.1 us (97%)
  between operations  0.64 us (3%)
    pallas_call x1, Pallas kernels, body(): pl.pallas_call(functools.partial(kernel, n, m, order.shape[0], chunks), o...  21.2 us
    pallas_call x1, Pallas kernels, body(): pl.pallas_call(hand_over, out_shape=tuple((jax.ShapeDtypeStruct(x.shape,...  0.92 us

profile of v4, /device:TPU:25, one launch (start us, length us, event | category | flops | bytes accessed | tf_op | source)
XLA Modules:
  0.0 22.8 jit_solution(12298994376616647387)
XLA Ops:
  0.6 21.2 %shard_map.76 = (bf16[64,4096]{1,0:T(8,128)(2,1)S(1)}, bf16[64,1024]{1,0:T(8,128)(2,1)S(1)}, bf16[64,1024]{1,0:T(8,128)(2,1)S(1)}) custom-call(s32[32]{0:T(128)} %order_hbm.1, bf16[64,4096]{1,0:T(8,128)(2,1)} %q_hbm.1, bf16[64,1024]{1,0:T(8,128)(2,1)} %k_hbm.1, bf16[64,1024]{1,0:T(8,128)(2,1)} %v_hbm.1, bf16[64,4096]{1,0:T(8,128)(2,1)} %g_hbm.1), custom_call_target="tpu_custom_call" | custom-call | tf_op jit(solution)/shard_map/pallas_call | solution.py:331
  21.9 0.9 %shard_map.77 = (bf16[64,4096]{1,0:T(8,128)(2,1)}, bf16[64,1024]{1,0:T(8,128)(2,1)}, bf16[64,1024]{1,0:T(8,128)(2,1)}) custom-call(bf16[64,4096]{1,0:T(8,128)(2,1)S(1)} %get-tuple-element.6.a, bf16[64,1024]{1,0:T(8,128)(2,1)S(1)} %get-tuple-element.7.b, bf16[64,1024]{1,0:T(8,128)(2,1)S(1)} %get-tuple-element.8.c), custom_call_target="tpu_custom_call" | custom-call | tf_op jit(solution)/shard_map/pallas_call | solution.py:374

commit v5 on v3

--- a/solution.py
+++ b/solution.py
@@ -131,6 +131,9 @@
         for d in range(1, n):
             to_part(d, c, False).start()
         to_near(c).start()
+    for c in range(min(2, chunks)):
+        for d in range(1, n):
+            to_part(d, c, True).start()
 
     loads[4].wait()
     mine = order[head * m + blk]
@@ -237,7 +240,8 @@
         for d in range(1, n):
             to_part(d, c, False).wait_recv()
             to_far(d, c).start()
-            to_part(d, c, True).start()
+            if c + 2 < chunks:
+                to_part(d, c + 2, True).start()
         if c == 0:
             loads[2].wait()
             loads[3].wait()

time: 22.2 us -> 21.5 us (0.968)
  Pallas kernels: 21.4 us -> 20.7 us
    pallas_call x1, Pallas kernels: 20.5 us -> 19.8 us  [body(): pl.pallas_call(functools.partial(kernel, n, m, order.shape[0], chunks), o...]
where the time goes in v5:
time: 21.5 us; the launch traced here: 21.4 us
  Pallas kernels  20.7 us (96%)
  between operations  0.64 us (3%)
    pallas_call x1, Pallas kernels, body(): pl.pallas_call(functools.partial(kernel, n, m, order.shape[0], chunks), o...  19.8 us
    pallas_call x1, Pallas kernels, body(): pl.pallas_call(hand_over, out_shape=tuple((jax.ShapeDtypeStruct(x.shape,...  0.92 us

profile of v5, /device:TPU:0, one launch (start us, length us, event | category | flops | bytes accessed | tf_op | source)
XLA Modules:
  0.0 21.4 jit_solution(739386850875491519)
XLA Ops:
  0.6 19.8 %shard_map.76 = (bf16[64,4096]{1,0:T(8,128)(2,1)S(1)}, bf16[64,1024]{1,0:T(8,128)(2,1)S(1)}, bf16[64,1024]{1,0:T(8,128)(2,1)S(1)}) custom-call(s32[32]{0:T(128)} %order_hbm.1, bf16[64,4096]{1,0:T(8,128)(2,1)} %q_hbm.1, bf16[64,1024]{1,0:T(8,128)(2,1)} %k_hbm.1, bf16[64,1024]{1,0:T(8,128)(2,1)} %v_hbm.1, bf16[64,4096]{1,0:T(8,128)(2,1)} %g_hbm.1), custom_call_target="tpu_custom_call" | custom-call | tf_op jit(solution)/shard_map/pallas_call | solution.py:335
  20.4 0.9 %shard_map.77 = (bf16[64,4096]{1,0:T(8,128)(2,1)}, bf16[64,1024]{1,0:T(8,128)(2,1)}, bf16[64,1024]{1,0:T(8,128)(2,1)}) custom-call(bf16[64,4096]{1,0:T(8,128)(2,1)S(1)} %get-tuple-element.6.a, bf16[64,1024]{1,0:T(8,128)(2,1)S(1)} %get-tuple-element.7.b, bf16[64,1024]{1,0:T(8,128)(2,1)S(1)} %get-tuple-element.8.c), custom_call_target="tpu_custom_call" | custom-call | tf_op jit(solution)/shard_map/pallas_call | solution.py:378

commit v6 on v5

--- a/solution.py
+++ b/solution.py
@@ -207,16 +207,6 @@
         weights_first = weights_first.astype(jnp.bfloat16)
         weights_rest = weights_rest.astype(jnp.bfloat16)
 
-        query_first = cols_dot(slopes_first, key_first)
-        query_rest = cols_dot(slopes_rest, key_rest)
-        query_grad = (
-            jnp.concatenate([query_first[:lanes], query_first[lanes:] + query_rest], axis=0)
-            * scale
-        ).astype(jnp.bfloat16)
-        for k in range(group):
-            out = pl.ds((kv_head * group + k) * HD, HD)
-            dq[lo, out] = query_grad[k * half : (k + 1) * half]
-            dq[hi, out] = query_grad[lanes + k * half : lanes + (k + 1) * half]
         grads_first = (
             plain_dot(slopes_first, queries) * scale,
             plain_dot(weights_first, grads),
@@ -236,6 +226,20 @@
                 at = (n + d) * half
                 prev_out[d, i, :, cols] = grads_rest[i][at : at + half].astype(jnp.bfloat16)
 
+        def query_side():
+            query_first = cols_dot(slopes_first, key_first)
+            query_rest = cols_dot(slopes_rest, key_rest)
+            query_grad = (
+                jnp.concatenate([query_first[:lanes], query_first[lanes:] + query_rest], axis=0)
+                * scale
+            ).astype(jnp.bfloat16)
+            for k in range(group):
+                out = pl.ds((kv_head * group + k) * HD, HD)
+                dq[lo, out] = query_grad[k * half : (k + 1) * half]
+                dq[hi, out] = query_grad[lanes + k * half : lanes + (k + 1) * half]
+
+        return query_side
+
     def stage_arrive(c):
         for d in range(1, n):
             to_part(d, c, False).wait_recv()
@@ -253,11 +257,12 @@
         for d in range(1, n):
             to_far(d, c).wait_recv()
             to_part(d, c, True).wait_recv()
-        for index in range(heads_in):
-            one_head(c * heads_in + index)
+        query_sides = [one_head(c * heads_in + index) for index in range(heads_in)]
         to_prev(c).start()
         for d in range(1, n):
             to_late(d, c).start()
+        for query_side in query_sides:
+            query_side()
         dq_copy(c).start()
 
     def stage_front(c):

time: 21.5 us -> 21.4 us (level)
  no operation moved by 1% of the time
where the time goes in v6:
time: 21.4 us; the launch traced here: 21.3 us
  Pallas kernels  20.7 us (97%)
  between operations  0.64 us (3%)
    pallas_call x1, Pallas kernels, body(): pl.pallas_call(functools.partial(kernel, n, m, order.shape[0], chunks), o...  19.7 us
    pallas_call x1, Pallas kernels, body(): pl.pallas_call(hand_over, out_shape=tuple((jax.ShapeDtypeStruct(x.shape,...  0.92 us

profile of v6, /device:TPU:0, one launch (start us, length us, event | category | flops | bytes accessed | tf_op | source)
XLA Modules:
  0.0 21.3 jit_solution(5193374011576363576)
XLA Ops:
  0.6 19.7 %shard_map.76 = (bf16[64,4096]{1,0:T(8,128)(2,1)S(1)}, bf16[64,1024]{1,0:T(8,128)(2,1)S(1)}, bf16[64,1024]{1,0:T(8,128)(2,1)S(1)}) custom-call(s32[32]{0:T(128)} %order_hbm.1, bf16[64,4096]{1,0:T(8,128)(2,1)} %q_hbm.1, bf16[64,1024]{1,0:T(8,128)(2,1)} %k_hbm.1, bf16[64,1024]{1,0:T(8,128)(2,1)} %v_hbm.1, bf16[64,4096]{1,0:T(8,128)(2,1)} %g_hbm.1), custom_call_target="tpu_custom_call" | custom-call | tf_op jit(solution)/shard_map/pallas_call | solution.py:340
  20.4 0.9 %shard_map.77 = (bf16[64,4096]{1,0:T(8,128)(2,1)}, bf16[64,1024]{1,0:T(8,128)(2,1)}, bf16[64,1024]{1,0:T(8,128)(2,1)}) custom-call(bf16[64,4096]{1,0:T(8,128)(2,1)S(1)} %get-tuple-element.6.a, bf16[64,1024]{1,0:T(8,128)(2,1)S(1)} %get-tuple-element.7.b, bf16[64,1024]{1,0:T(8,128)(2,1)S(1)} %get-tuple-element.8.c), custom_call_target="tpu_custom_call" | custom-call | tf_op jit(solution)/shard_map/pallas_call | solution.py:383

commit v7 on v6

--- a/solution.py
+++ b/solution.py
@@ -82,10 +82,9 @@
             sends.at[d - 1, c], recvs.at[d - 1, c], up[d],
         )
 
-    def to_near(c):
-        return remote(
-            kv.at[:, pl.ds(0, half), span(c)], early.at[0, :, :, span(c)],
-            near_s.at[c], near_r.at[c], ahead,
+    def to_near():
+        return remote(
+            kv.at[:, pl.ds(0, half)], early.at[0], near_s.at[0], near_r.at[0], ahead
         )
 
     def to_far(d, c):
@@ -130,7 +129,8 @@
     for c in range(chunks):
         for d in range(1, n):
             to_part(d, c, False).start()
-        to_near(c).start()
+        if c == 0:
+            to_near().start()
     for c in range(min(2, chunks)):
         for d in range(1, n):
             to_part(d, c, True).start()
@@ -253,7 +253,8 @@
             first_logits(c * heads_in + index)
 
     def stage_compute(c):
-        to_near(c).wait_recv()
+        if c == 0:
+            to_near().wait_recv()
         for d in range(1, n):
             to_far(d, c).wait_recv()
             to_part(d, c, True).wait_recv()
@@ -298,7 +299,8 @@
     for c in range(chunks):
         stage_finish(c)
     for c in range(chunks):
-        to_near(c).wait_send()
+        if c == 0:
+            to_near().wait_send()
         to_prev(c).wait_send()
         for d in range(1, n):
             to_part(d, c, False).wait_send()

time: 21.4 us -> 21.4 us (level)
  no operation moved by 1% of the time
where the time goes in v7:
time: 21.4 us; the launch traced here: 21.3 us
  Pallas kernels  20.6 us (96%)
  between operations  0.64 us (3%)
    pallas_call x1, Pallas kernels, body(): pl.pallas_call(functools.partial(kernel, n, m, order.shape[0], chunks), o...  19.7 us
    pallas_call x1, Pallas kernels, body(): pl.pallas_call(hand_over, out_shape=tuple((jax.ShapeDtypeStruct(x.shape,...  0.92 us

profile of v7, /device:TPU:0, one launch (start us, length us, event | category | flops | bytes accessed | tf_op | source)
XLA Modules:
  0.0 21.3 jit_solution(10365333117228762652)
XLA Ops:
  0.6 19.7 %shard_map.76 = (bf16[64,4096]{1,0:T(8,128)(2,1)S(1)}, bf16[64,1024]{1,0:T(8,128)(2,1)S(1)}, bf16[64,1024]{1,0:T(8,128)(2,1)S(1)}) custom-call(s32[32]{0:T(128)} %order_hbm.1, bf16[64,4096]{1,0:T(8,128)(2,1)} %q_hbm.1, bf16[64,1024]{1,0:T(8,128)(2,1)} %k_hbm.1, bf16[64,1024]{1,0:T(8,128)(2,1)} %v_hbm.1, bf16[64,4096]{1,0:T(8,128)(2,1)} %g_hbm.1), custom_call_target="tpu_custom_call" | custom-call | tf_op jit(solution)/shard_map/pallas_call | solution.py:342
  20.4 0.9 %shard_map.77 = (bf16[64,4096]{1,0:T(8,128)(2,1)}, bf16[64,1024]{1,0:T(8,128)(2,1)}, bf16[64,1024]{1,0:T(8,128)(2,1)}) custom-call(bf16[64,4096]{1,0:T(8,128)(2,1)S(1)} %get-tuple-element.6.a, bf16[64,1024]{1,0:T(8,128)(2,1)S(1)} %get-tuple-element.7.b, bf16[64,1024]{1,0:T(8,128)(2,1)S(1)} %get-tuple-element.8.c), custom_call_target="tpu_custom_call" | custom-call | tf_op jit(solution)/shard_map/pallas_call | solution.py:385
